TPU v7x, 128 devices: a whole 4x4x4 slice. The times are simulated.
128 devices in a mesh: depth: 8 (over y, z_hi), chan: 16 (over z_lo, x, core).
Axes of the slice: x: 4, y: 4, z: 4 (z_hi: 2, z_lo: 2; z = z_hi * 2 + z_lo), core: 2. Of those that a mesh axis runs over, the one named last changes fastest.
Arguments:
- volume: bfloat16 [256, 32, 4096], P('chan', 'depth'), may hold values from -6 to 6
- kernel: bfloat16 [27, 256, 512], P(None, 'chan'), may hold values from -0.109375 to 0.109375
- cotangent: bfloat16 [512, 16, 1024], P('chan', 'depth'), may hold values from -6 to 6
Outputs:
- activated: bfloat16 [512, 16, 1024], P('chan', 'depth')
- grad_volume: bfloat16 [256, 32, 4096], P('chan', 'depth')
- grad_kernel: float32 [27, 256, 512], P(None, 'chan')
All inputs are finite; a program needn't handle non-finite values.
Results may differ from a plain program's by a relative error of at most 0.005.
Values may be sent and summed in bfloat16 or wider, within the bound.
A program may use at most 192 MiB of HBM per device.

v0:
```python
import itertools

import jax
import jax.numpy as jnp
from jax import lax
from jax.experimental import pallas as pl
from jax.experimental.pallas import tpu as pltpu
from jax.sharding import PartitionSpec as P

MESH = pl.DeviceIdType.MESH
BF = jnp.bfloat16
F32 = jnp.float32
SIDE = 32
CELLS = SIDE * SIDE
TAPS = 27
INS = 16
OUTS = 32
ROWS = TAPS * INS
LEVEL = 9 * INS
DEEP = 512
ALL = 512
PIECE = 112
COPIES = 80


def tap_phase(offset):
    if offset == 1:
        return (0, 0)
    if offset == 2:
        return (1, 0)
    return (1, -1)


def taps_2d():
    for row in range(3):
        for col in range(3):
            row_phase, row_step = tap_phase(row)
            col_phase, col_step = tap_phase(col)
            yield 3 * row + col, 2 * row_phase + col_phase, row_step, col_step


def inside(row_step, col_step):
    places = lax.broadcasted_iota(jnp.int32, (INS, CELLS), 1)
    keep = None
    if row_step:
        keep = places >= SIDE
    if col_step:
        col = (places % SIDE) != 0
        keep = col if keep is None else keep & col
    return keep


def dot(left, right, contract):
    return lax.dot_general(left, right, (contract, ((), ())), preferred_element_type=F32)


def body(
    vol, wk, cot, act, gvol, gker,
    low, upper, views, wfull, wt, sib_out, sib_in, acc,
    a1_out, a1_in, a2_out, a2_in, a3_out, a3_in,
    b1_out, b1_in, b2_out, b2_in, b3_out, b3_in,
    grads, back_out, filt, c1_out, c1_in, c2_out, c2_in, c3_out, c3_in, gk16,
    send_sem, recv_sem,
):
    depth = lax.axis_index("depth")
    chan = lax.axis_index("chan")
    y, zh = depth // 2, depth % 2
    zl, x, core = chan // 8, (chan // 2) % 4, chan % 2

    def at_chan(zl_, x_, core_):
        return (depth, zl_ * 8 + x_ * 2 + core_)

    sibling = at_chan(zl, x, 1 - core)
    right = at_chan(zl, (x + 1) % 4, core)
    left = at_chan(zl, (x + 3) % 4, core)
    pair = at_chan(1 - zl, x, core)
    y_right = (((y + 1) % 4) * 2 + zh, chan)
    y_left = (((y + 3) % 4) * 2 + zh, chan)
    y_pair = (y * 2 + 1 - zh, chan)
    above = ((depth + 1) % 8, chan)
    below = ((depth + 7) % 8, chan)
    peers = (sibling, right, left, pair, y_right, y_left, y_pair, above, below)

    barrier = pltpu.get_barrier_semaphore()
    for peer in peers:
        pl.semaphore_signal(barrier, inc=1, device_id=peer, device_id_type=MESH)

    number = itertools.count()
    sent = []

    def push(src, dst, target):
        n = next(number)
        copy = pltpu.make_async_remote_copy(
            src_ref=src, dst_ref=dst, send_sem=send_sem.at[n], recv_sem=recv_sem.at[n],
            device_id=target, device_id_type=MESH,
        )
        copy.start()
        sent.append(copy)
        return copy

    def build(level, plane):
        wide = plane.astype(F32)
        for tap, phase, row_step, col_step in taps_2d():
            view = wide[:, phase * CELLS : (phase + 1) * CELLS]
            amount = -row_step * SIDE - col_step
            if amount:
                view = jnp.where(inside(row_step, col_step), pltpu.roll(view, amount, 1), 0.0)
            start = level * LEVEL + tap * INS
            views[start : start + INS, :] = view.astype(BF)

    wfull[0:ROWS, :] = wk[...]
    wfull[ROWS:DEEP, :] = jnp.zeros((DEEP - ROWS, ALL), BF)
    wfull[...] = wfull[...].T
    for far in range(2):
        for z_rel in range(2):
            for x_rel in range(4):
                block = ((zl + z_rel) % 2) * 8 + ((x + x_rel) % 4) * 2 + (core + far) % 2
                rows = pl.ds(pl.multiple_of(block * OUTS, OUTS), OUTS)
                start = (z_rel * 4 + x_rel) * OUTS
                wt[far, start : start + OUTS, :] = wfull[rows, :]

    pl.semaphore_wait(barrier, len(peers))
    halo = push(vol.at[3], low, above)

    views[5 * LEVEL :, :] = jnp.zeros((views.shape[0] - 5 * LEVEL, CELLS), BF)
    for plane in (1, 2, 3):
        build(plane + 1, vol[plane])

    def partial(q, far):
        first = 2 * LEVEL * q
        return dot(wt[far], views[first : first + DEEP, :], ((1,), (0,)))

    sib_out[1] = partial(1, 1).astype(BF)
    sib_1 = push(sib_out.at[1], sib_in.at[1], sibling)
    acc[1] = partial(1, 0)
    build(1, vol[0])
    halo.wait_recv()
    build(0, jnp.where(depth > 0, low[...], jnp.zeros((), BF)))
    sib_out[0] = partial(0, 1).astype(BF)
    sib_0 = push(sib_out.at[0], sib_in.at[0], sibling)

    def rows_of(z_rel, x_rel):
        start = (z_rel * 4 + x_rel) * OUTS
        return slice(start, start + OUTS)

    sib_1.wait_recv()
    acc[1] = acc[1] + sib_in[1].astype(F32)
    a1_out[0] = acc[1, rows_of(0, 2), :].astype(BF)
    a1_out[1] = acc[1, rows_of(1, 2), :].astype(BF)
    a1_r = push(a1_out.at[0], a1_in.at[0], right)
    a1_l = push(a1_out.at[1], a1_in.at[1], left)
    acc[0] = partial(0, 0)
    sib_0.wait_recv()
    half = 4 * OUTS
    b1_out[...] = (acc[0, half:, :] + sib_in[0, half:, :].astype(F32)).astype(BF)
    b1 = push(b1_out, b1_in, pair)
    acc[0, :half, :] = acc[0, :half, :] + sib_in[0, :half, :].astype(F32)
    a1_r.wait_recv()
    a2_out[0, 0] = (acc[1, rows_of(0, 1), :] + a1_in[0].astype(F32)).astype(BF)
    a2_out[0, 1] = acc[1, rows_of(1, 1), :].astype(BF)
    a2_r = push(a2_out.at[0], a2_in.at[0], right)
    a1_l.wait_recv()
    a2_out[1, 0] = acc[1, rows_of(0, 3), :].astype(BF)
    a2_out[1, 1] = (acc[1, rows_of(1, 3), :] + a1_in[1].astype(F32)).astype(BF)
    a2_l = push(a2_out.at[1], a2_in.at[1], left)
    a2_r.wait_recv()
    a2_l.wait_recv()
    a3_out[...] = (
        acc[1, rows_of(1, 0), :] + a2_in[0, 1].astype(F32) + a2_in[1, 1].astype(F32)
    ).astype(BF)
    a3 = push(a3_out, a3_in, pair)
    b1.wait_recv()
    acc[0, :half, :] = acc[0, :half, :] + b1_in[...].astype(F32)
    cut = OUTS // 2
    b2_out[0] = acc[0, 2 * OUTS : 2 * OUTS + cut, :].astype(BF)
    b2_out[1] = acc[0, 2 * OUTS + cut : 3 * OUTS, :].astype(BF)
    b2_r = push(b2_out.at[0], b2_in.at[0], right)
    b2_l = push(b2_out.at[1], b2_in.at[1], left)
    b2_r.wait_recv()
    b3_out[0, :cut, :] = (acc[0, OUTS : OUTS + cut, :] + b2_in[0].astype(F32)).astype(BF)
    b3_out[0, cut:, :] = acc[0, OUTS + cut : 2 * OUTS, :].astype(BF)
    b3_r = push(b3_out.at[0], b3_in.at[0], right)
    b2_l.wait_recv()
    b3_out[1, :cut, :] = acc[0, 3 * OUTS : 3 * OUTS + cut, :].astype(BF)
    b3_out[1, cut:, :] = (acc[0, 3 * OUTS + cut : 4 * OUTS, :] + b2_in[1].astype(F32)).astype(BF)
    b3_l = push(b3_out.at[1], b3_in.at[1], left)

    def rows_abs(zl_, x_, core_):
        return pl.multiple_of((zl_ * 8 + x_ * 2 + core_) * OUTS, OUTS)

    mine = rows_abs(zl, x, core)

    def activate(q, preact):
        s = 1.0 / (1.0 + jnp.exp(-preact))
        act[q] = (preact * s).astype(BF)
        grad = cot[q].astype(F32) * s * (1.0 + preact * (1.0 - s))
        grads[q, pl.ds(mine, OUTS), :] = grad.astype(BF)

    def spread(q, start, target, rows=OUTS, skip=0):
        place = grads.at[q, pl.ds(pl.multiple_of(start + skip, 16), rows), :]
        return push(place, place, target)

    xl, xr, xo, zo = (x + 3) % 4, (x + 1) % 4, (x + 2) % 4, 1 - zl
    from_sib = []

    def share(q, start):
        from_sib.append(spread(q, start, sibling))

    a3.wait_recv()
    activate(1, acc[1, rows_of(0, 0), :] + a2_in[0, 0].astype(F32) + a2_in[1, 0].astype(F32) + a3_in[...].astype(F32))
    g1_r = spread(1, mine, right)
    g1_l = spread(1, mine, left)
    g1_z = [spread(1, mine, pair)]
    share(1, mine)
    b3_r.wait_recv()
    b3_l.wait_recv()
    activate(0, acc[0, :OUTS, :] + b3_in[0].astype(F32) + b3_in[1].astype(F32))
    g0_z = spread(0, mine, pair)
    g0_r = spread(0, mine, right)
    g0_l = spread(0, mine, left)
    share(0, mine)

    g1_r.wait_recv()
    block = rows_abs(zl, xl, core)
    g1_fr = spread(1, block, right, cut)
    g1_z.append(spread(1, block, pair))
    share(1, block)
    g1_l.wait_recv()
    block = rows_abs(zl, xr, core)
    g1_fl = spread(1, block, left, cut, cut)
    g1_z.append(spread(1, block, pair))
    share(1, block)
    g0_z.wait_recv()
    block = rows_abs(zo, x, core)
    g0_zr = spread(0, block, right)
    g0_zl = spread(0, block, left)
    share(0, block)
    g0_r.wait_recv()
    block = rows_abs(zl, xl, core)
    g0_fr = spread(0, block, right)
    share(0, block)
    g0_l.wait_recv()
    share(0, rows_abs(zl, xr, core))
    g1_fr.wait_recv()
    g1_fl.wait_recv()
    block = rows_abs(zl, xo, core)
    g1_z.append(spread(1, block, pair))
    share(1, block)
    g0_zr.wait_recv()
    share(0, rows_abs(zo, xl, core))
    g0_zl.wait_recv()
    block = rows_abs(zo, xr, core)
    g0_fl = spread(0, block, left)
    share(0, block)
    g0_fr.wait_recv()
    share(0, rows_abs(zl, xo, core))
    g0_fl.wait_recv()
    share(0, rows_abs(zo, xo, core))
    for copy, x_ in zip(g1_z, (x, xl, xr, xo)):
        copy.wait_recv()
        share(1, rows_abs(zo, x_, core))
    for copy in from_sib:
        copy.wait_recv()

    def spatial(columns):
        sums = {}
        for tap, phase, row_step, col_step in taps_2d():
            moved = columns[tap * INS : (tap + 1) * INS, :]
            amount = -row_step * SIDE - col_step
            if amount:
                moved = pltpu.roll(jnp.where(inside(row_step, col_step), moved, 0.0), CELLS - amount, 1)
            sums[phase] = moved if phase not in sums else sums[phase] + moved
        return [sums[phase] for phase in range(4)]

    def columns_of(q, level):
        return spatial(dot(wk[level * LEVEL : (level + 1) * LEVEL, :], grads[q], ((1,), (0,))))

    def phase_cells(phase):
        return slice(phase * CELLS, (phase + 1) * CELLS)

    lowest = columns_of(0, 0)
    for phase in range(4):
        back_out[:, phase_cells(phase)] = lowest[phase].astype(BF)
    back = push(back_out, upper, below)

    filt[0:ROWS, :] = dot(views[0:ROWS, :], grads[0], ((1,), (1,))) + dot(
        views[2 * LEVEL : 2 * LEVEL + ROWS, :], grads[1], ((1,), (1,))
    )
    filt[ROWS:, :] = jnp.zeros((filt.shape[0] - ROWS, ALL), F32)

    def piece(y_rel, part):
        start = pl.multiple_of(((y + y_rel) % 4) * PIECE, PIECE)
        return filt[pl.ds(start, PIECE), part * 256 : part * 256 + 256]

    c1_out[0] = piece(2, 0).astype(BF)
    c1_out[1] = piece(2, 1).astype(BF)
    c1_r = push(c1_out.at[0], c1_in.at[0], y_right)
    c1_l = push(c1_out.at[1], c1_in.at[1], y_left)

    def store_plane(plane, parts, more=None):
        for phase in range(4):
            total = parts[phase] if more is None else parts[phase] + more[phase]
            gvol[plane, :, phase_cells(phase)] = total.astype(BF)

    store_plane(0, columns_of(0, 1))
    c1_r.wait_recv()
    c2_out[0, 0] = (piece(1, 0) + c1_in[0].astype(F32)).astype(BF)
    c2_out[0, 1] = piece(1, 1).astype(BF)
    c2_r = push(c2_out.at[0], c2_in.at[0], y_right)
    c1_l.wait_recv()
    c2_out[1, 0] = piece(3, 0).astype(BF)
    c2_out[1, 1] = (piece(3, 1) + c1_in[1].astype(F32)).astype(BF)
    c2_l = push(c2_out.at[1], c2_in.at[1], y_left)
    store_plane(1, columns_of(0, 2), columns_of(1, 0))
    store_plane(2, columns_of(1, 1))
    c2_r.wait_recv()
    c2_l.wait_recv()
    whole = [piece(0, part) + c2_in[0, part].astype(F32) + c2_in[1, part].astype(F32) for part in range(2)]
    c3_out[...] = jnp.where(zh == 0, whole[1], whole[0]).astype(BF)
    c3 = push(c3_out, c3_in, y_pair)
    own = jnp.where(zh == 0, whole[0], whole[1])
    last = columns_of(1, 2)
    back.wait_recv()
    edge = upper[...].astype(F32)
    edge = jnp.where(depth < 7, edge, 0.0)
    store_plane(3, last, [edge[:, phase_cells(phase)] for phase in range(4)])
    c3.wait_recv()
    gk16[y, zh] = (own + c3_in[...].astype(F32)).astype(BF)

    def pass_on(y_, part, target):
        return push(gk16.at[y_, part], gk16.at[y_, part], target)

    yl, yr, yo = (y + 3) % 4, (y + 1) % 4, (y + 2) % 4
    d_z = pass_on(y, zh, y_pair)
    d_r = pass_on(y, zh, y_right)
    d_l = pass_on(y, zh, y_left)
    d_z.wait_recv()
    e_r = pass_on(y, 1 - zh, y_right)
    e_l = pass_on(y, 1 - zh, y_left)
    d_r.wait_recv()
    f_r = pass_on(yl, zh, y_right)
    d_l.wait_recv()
    e_r.wait_recv()
    e_l.wait_recv()
    f_l = pass_on(yr, 1 - zh, y_left)
    f_r.wait_recv()
    f_l.wait_recv()
    for y_ in range(4):
        rows = min(PIECE, ROWS - y_ * PIECE)
        for part in range(2):
            gker[y_ * PIECE : y_ * PIECE + rows, part * 256 : part * 256 + 256] = gk16[y_, part, :rows, :].astype(F32)
    for copy in sent:
        copy.wait_send()


def on_device(volume, kernel, cotangent):
    planes = volume.transpose(1, 0, 2)
    upstream = cotangent.transpose(1, 0, 2)
    vmem = pl.BlockSpec(memory_space=pltpu.VMEM)
    scratch = [
        ((INS, 4 * CELLS), BF),
        ((INS, 4 * CELLS), BF),
        ((2 * LEVEL + DEEP, CELLS), BF),
        ((ALL, DEEP), BF),
        ((2, ALL // 2, DEEP), BF),
        ((2, ALL // 2, CELLS), BF),
        ((2, ALL // 2, CELLS), BF),
        ((2, ALL // 2, CELLS), F32),
        ((2, OUTS, CELLS), BF),
        ((2, OUTS, CELLS), BF),
        ((2, 2, OUTS, CELLS), BF),
        ((2, 2, OUTS, CELLS), BF),
        ((OUTS, CELLS), BF),
        ((OUTS, CELLS), BF),
        ((4 * OUTS, CELLS), BF),
        ((4 * OUTS, CELLS), BF),
        ((2, OUTS // 2, CELLS), BF),
        ((2, OUTS // 2, CELLS), BF),
        ((2, OUTS, CELLS), BF),
        ((2, OUTS, CELLS), BF),
        ((2, ALL, CELLS), BF),
        ((INS, 4 * CELLS), BF),
        ((4 * PIECE, ALL), F32),
        ((2, PIECE, 256), BF),
        ((2, PIECE, 256), BF),
        ((2, 2, PIECE, 256), BF),
        ((2, 2, PIECE, 256), BF),
        ((PIECE, 256), BF),
        ((PIECE, 256), BF),
        ((4, 2, PIECE, 256), BF),
    ]
    activated, grad_volume, grad_kernel = pl.pallas_call(
        body,
        out_shape=(
            jax.ShapeDtypeStruct((2, OUTS, CELLS), BF),
            jax.ShapeDtypeStruct((4, INS, 4 * CELLS), BF),
            jax.ShapeDtypeStruct((ROWS, ALL), F32),
        ),
        in_specs=[vmem] * 3,
        out_specs=(vmem,) * 3,
        scratch_shapes=[pltpu.VMEM(shape, kind) for shape, kind in scratch]
        + [pltpu.SemaphoreType.DMA((COPIES,)), pltpu.SemaphoreType.DMA((COPIES,))],
        compiler_params=pltpu.CompilerParams(
            collective_id=0, has_side_effects=True, vmem_limit_bytes=48 * 1024 * 1024
        ),
    )(planes, kernel.reshape(ROWS, ALL), upstream)
    return (
        activated.transpose(1, 0, 2),
        grad_volume.transpose(1, 0, 2),
        grad_kernel.reshape(TAPS, INS, ALL),
    )


def solution(mesh):
    return jax.shard_map(
        on_device,
        mesh=mesh,
        in_specs=(P("chan", "depth", None), P(None, "chan", None), P("chan", "depth", None)),
        out_specs=(P("chan", "depth", None), P("chan", "depth", None), P(None, "chan", None)),
        check_vma=False,
    )
```

profile of v0, /device:TPU:4, one launch (start us, length us, event | category | flops | bytes accessed | tf_op | source)
XLA Modules:
  0.0 73.0 jit_solution(7947822572995969269)
XLA Ops:
  0.6 0.9 %copy.13 = bf16[32,2,1024]{2,0,1:T(8,128)(2,1)S(1)} copy(bf16[32,2,1024]{2,1,0:T(2,128)(2,1)} %param.5) | data formatting | bytes 262144 | tf_op args[2]
  1.6 0.0 copy-start
  1.6 1.4 %copy.12 = bf16[16,4,4096]{2,0,1:T(8,128)(2,1)S(1)} copy(bf16[16,4,4096]{2,1,0:T(4,128)(2,1)} %param.3) | data formatting | bytes 1048576 | tf_op args[0]
  3.0 0.0 copy-done
  3.0 67.1 %shard_map.58 = (bf16[2,32,1024]{2,1,0:T(8,128)(2,1)S(1)}, bf16[4,16,4096]{2,1,0:T(8,128)(2,1)S(1)}, f32[432,512]{1,0:T(8,128)S(1)}) custom-call(bf16[4,16,4096]{2,1,0:T(8,128)(2,1)S(1)} %bitcast.10, bf16[432,512]{1,0:T(8,128)(2,1)S(1)} %bitcast.14, bf16[2,32,1024]{2,1,0:T(8,128)(2,1)S(1)} %bitcast.12), custom_call_target="tpu_custom_call" | custom-call | tf_op jit(solution)/shard_map/pallas_call | solution.py:392
  70.0 0.8 %copy.8 = bf16[32,2,1024]{2,1,0:T(2,128)(2,1)} copy(bf16[32,2,1024]{2,0,1:T(8,128)(2,1)S(1)} %bitcast.15) | data formatting | bytes 262144
  70.8 1.2 %copy.9 = bf16[16,4,4096]{2,1,0:T(4,128)(2,1)} copy(bf16[16,4,4096]{2,0,1:T(8,128)(2,1)S(1)} %bitcast.13) | data formatting | bytes 1048576
  72.0 0.9 %copy.15 = f32[27,16,512]{2,1,0:T(8,128)} copy(f32[27,16,512]{2,1,0:T(8,128)S(1)} %bitcast.11) | data formatting | bytes 1769472
Async XLA Ops:
  1.6 1.4 %copy-start = (bf16[27,16,512]{2,1,0:T(8,128)(2,1)S(1)}, bf16[27,16,512]{2,1,0:T(8,128)(2,1)}, u32[]{:S(2)}) copy-start(bf16[27,16,512]{2,1,0:T(8,128)(2,1)} %param.4) | copy-start | bytes 1327108
where the time goes:
time: 73.1 us; the launch traced here: 73 us
  Pallas kernels  67.1 us (92%)
  local copies, waits for them, and re-layouts  5.23 us (7%)
    pallas_call x1, Pallas kernels, on_device(): pl.pallas_call(body, out_shape=(jax.ShapeDtypeStruct((2, OUTS, CELLS), BF...  67.1 us
    unnamed x7, local copies, waits for them, and re-layouts  5.23 us

commit v1 on v0

v1 whole, which is shorter than its diff:
```python
import itertools

import jax
import jax.numpy as jnp
from jax import lax
from jax.experimental import pallas as pl
from jax.experimental.pallas import tpu as pltpu
from jax.sharding import PartitionSpec as P

MESH = pl.DeviceIdType.MESH
BF = jnp.bfloat16
F32 = jnp.float32
SIDE = 32
CELLS = SIDE * SIDE
TAPS = 27
INS = 16
OUTS = 32
ROWS = TAPS * INS
LEVEL = 9 * INS
DEEP = 512
ALL = 512
HALF = ALL // 2
PIECE = 112
PART = 128
COPIES = 80


def tap_phase(offset):
    if offset == 1:
        return (0, 0)
    if offset == 2:
        return (1, 0)
    return (1, -1)


def taps_2d():
    for row in range(3):
        for col in range(3):
            row_phase, row_step = tap_phase(row)
            col_phase, col_step = tap_phase(col)
            yield 3 * row + col, 2 * row_phase + col_phase, row_step, col_step


def inside(row_step, col_step):
    places = lax.broadcasted_iota(jnp.int32, (INS, CELLS), 1)
    keep = None
    if row_step:
        keep = places >= SIDE
    if col_step:
        col = (places % SIDE) != 0
        keep = col if keep is None else keep & col
    return keep


def dot(left, right, contract):
    return lax.dot_general(left, right, (contract, ((), ())), preferred_element_type=F32)


def body(
    vol, wk, cot, act, gvol, gker,
    low, upper, views, wfull, wt, sib_out, sib_in, acc, rs_out, rs_in,
    grads, back_out, filt, filt_out, filt_in, gk16,
    send_sem, recv_sem,
):
    depth = lax.axis_index("depth")
    chan = lax.axis_index("chan")
    y, zh = depth // 2, depth % 2
    zl, x, core = chan // 8, (chan // 2) % 4, chan % 2

    def at_chan(dz, dx, dc=0):
        return (depth, ((zl + dz) % 2) * 8 + ((x + dx) % 4) * 2 + (core + dc) % 2)

    def at_depth(dz, dy):
        return (((y + dy) % 4) * 2 + (zh + dz) % 2, chan)

    near = [(0, 1), (0, 3), (0, 2)]
    far = [(1, 0), (1, 1), (1, 3), (1, 2)]
    moves = near + far
    sibling = at_chan(0, 0, 1)
    above = ((depth + 1) % 8, chan)
    below = ((depth + 7) % 8, chan)

    barrier = pltpu.get_barrier_semaphore()
    peers = [sibling] + [at_chan(*m) for m in moves] + [at_depth(*m) for m in moves]
    for peer in peers:
        pl.semaphore_signal(barrier, inc=1, device_id=peer, device_id_type=MESH)

    number = itertools.count()
    sent = []

    def push(src, dst, target):
        n = next(number)
        copy = pltpu.make_async_remote_copy(
            src_ref=src, dst_ref=dst, send_sem=send_sem.at[n], recv_sem=recv_sem.at[n],
            device_id=target, device_id_type=MESH,
        )
        copy.start()
        sent.append(copy)
        return copy

    def build(level, plane):
        wide = plane.astype(F32)
        for tap, phase, row_step, col_step in taps_2d():
            view = wide[:, phase * CELLS : (phase + 1) * CELLS]
            amount = -row_step * SIDE - col_step
            if amount:
                view = jnp.where(inside(row_step, col_step), pltpu.roll(view, amount, 1), 0.0)
            start = level * LEVEL + tap * INS
            views[start : start + INS, :] = view.astype(BF)

    wfull[0:ROWS, :] = wk[...]
    wfull[ROWS:DEEP, :] = jnp.zeros((DEEP - ROWS, ALL), BF)
    wfull[...] = wfull[...].T
    for other in range(2):
        for z_rel in range(2):
            for x_rel in range(4):
                block = ((zl + z_rel) % 2) * 8 + ((x + x_rel) % 4) * 2 + (core + other) % 2
                rows = pl.ds(pl.multiple_of(block * OUTS, OUTS), OUTS)
                start = (z_rel * 4 + x_rel) * OUTS
                wt[other, start : start + OUTS, :] = wfull[rows, :]

    pl.semaphore_wait(barrier, len(peers))
    halo = push(vol.at[3], low, above)

    views[5 * LEVEL :, :] = jnp.zeros((views.shape[0] - 5 * LEVEL, CELLS), BF)
    for plane in (1, 2, 3):
        build(plane + 1, vol[plane])

    def partial(q, other):
        first = 2 * LEVEL * q
        return dot(wt[other], views[first : first + DEEP, :], ((1,), (0,)))

    def to_sibling(q):
        sib_out[q] = partial(q, 1).astype(BF)
        return push(sib_out.at[q], sib_in.at[q], sibling)

    def scatter(q, copy):
        copy.wait_recv()
        acc[q] = acc[q] + sib_in[q].astype(F32)
        rs_out[q] = acc[q].astype(BF)
        copies = []
        for n, (dz, dx) in enumerate(moves):
            start = (dz * 4 + dx) * OUTS
            copies.append(push(rs_out.at[q, start : start + OUTS, :], rs_in.at[q, n], at_chan(dz, dx)))
        return copies

    sib_1 = to_sibling(1)
    acc[1] = partial(1, 0)
    scatter_1 = scatter(1, sib_1)
    build(1, vol[0])
    halo.wait_recv()
    build(0, jnp.where(depth > 0, low[...], jnp.zeros((), BF)))
    sib_0 = to_sibling(0)
    acc[0] = partial(0, 0)
    scatter_0 = scatter(0, sib_0)

    def rows_abs(dz, dx):
        return pl.multiple_of((((zl + dz) % 2) * 8 + ((x + dx) % 4) * 2 + core) * OUTS, OUTS)

    def activate(q, copies):
        for copy in copies:
            copy.wait_recv()
        preact = acc[q, 0:OUTS, :]
        for n in range(len(moves)):
            preact = preact + rs_in[q, n].astype(F32)
        s = 1.0 / (1.0 + jnp.exp(-preact))
        act[q] = (preact * s).astype(BF)
        grad = cot[q].astype(F32) * s * (1.0 + preact * (1.0 - s))
        grads[q, pl.ds(rows_abs(0, 0), OUTS), :] = grad.astype(BF)

    def spread(q, start, target):
        place = grads.at[q, pl.ds(start, OUTS), :]
        return push(place, place, target)

    def gather(q):
        copies = {move: spread(q, rows_abs(0, 0), at_chan(*move)) for move in moves}
        return copies, {(0, 0): spread(q, rows_abs(0, 0), sibling)}

    def share(q, gathered, group):
        for dz, dx in group:
            gathered[0][dz, dx].wait_recv()
            gathered[1][dz, dx] = spread(q, rows_abs(dz, -dx), sibling)

    activate(1, scatter_1)
    gathered_1 = gather(1)
    activate(0, scatter_0)
    gathered_0 = gather(0)
    share(1, gathered_1, near)
    share(1, gathered_1, far)
    share(0, gathered_0, near)
    for gathered in (gathered_1, gathered_0):
        for move in [(0, 0)] + near:
            gathered[1][move].wait_recv()

    def filters(part, z):
        columns = pl.ds(pl.multiple_of(z * HALF, HALF), HALF)
        total = dot(views[0:ROWS, :], grads[0, columns, :], ((1,), (1,))) + dot(
            views[2 * LEVEL : 2 * LEVEL + ROWS, :], grads[1, columns, :], ((1,), (1,))
        )
        for side in range(2):
            filt[part, side, 0:ROWS, :] = total[:, side * PART : (side + 1) * PART]
        filt[part, :, ROWS:, :] = jnp.zeros((2, 4 * PIECE - ROWS, PART), F32)
        filt_out[part] = filt[part].astype(BF)
        copies = []
        for n, (dz, dy) in enumerate(moves):
            start = pl.multiple_of(((y + dy) % 4) * PIECE, PIECE)
            src = filt_out.at[part, (zh + dz) % 2, pl.ds(start, PIECE), :]
            copies.append(push(src, filt_in.at[part, n], at_depth(dz, dy)))
        return copies

    def summed(part, copies):
        for copy in copies:
            copy.wait_recv()
        start = pl.multiple_of(y * PIECE, PIECE)
        total = filt[part, zh, pl.ds(start, PIECE), :]
        for n in range(len(moves)):
            total = total + filt_in[part, n].astype(F32)
        gk16[part, y, zh] = total.astype(BF)
        place = gk16.at[part, y, zh]
        return [push(place, place, at_depth(*move)) for move in moves]

    def finish(part, z, copies):
        for copy in copies:
            copy.wait_recv()
        for y_ in range(4):
            rows = min(PIECE, ROWS - y_ * PIECE)
            for side in range(2):
                columns = pl.ds(pl.multiple_of(z * HALF + side * PART, PART), PART)
                gker[y_ * PIECE : y_ * PIECE + rows, columns] = gk16[part, y_, side, :rows, :].astype(F32)

    reduce_0 = filters(0, zl)
    share(0, gathered_0, far)
    for gathered in (gathered_1, gathered_0):
        for move in far:
            gathered[1][move].wait_recv()
    reduce_1 = filters(1, 1 - zl)

    def spatial(columns):
        sums = {}
        for tap, phase, row_step, col_step in taps_2d():
            moved = columns[tap * INS : (tap + 1) * INS, :]
            amount = -row_step * SIDE - col_step
            if amount:
                moved = pltpu.roll(jnp.where(inside(row_step, col_step), moved, 0.0), CELLS - amount, 1)
            sums[phase] = moved if phase not in sums else sums[phase] + moved
        return [sums[phase] for phase in range(4)]

    def columns_of(q, level):
        return spatial(dot(wk[level * LEVEL : (level + 1) * LEVEL, :], grads[q], ((1,), (0,))))

    def phase_cells(phase):
        return slice(phase * CELLS, (phase + 1) * CELLS)

    def store_plane(plane, parts, more=None):
        for phase in range(4):
            total = parts[phase] if more is None else parts[phase] + more[phase]
            gvol[plane, :, phase_cells(phase)] = total.astype(BF)

    lowest = columns_of(0, 0)
    for phase in range(4):
        back_out[:, phase_cells(phase)] = lowest[phase].astype(BF)
    back = push(back_out, upper, below)
    spread_0 = summed(0, reduce_0)
    store_plane(0, columns_of(0, 1))
    store_plane(1, columns_of(0, 2), columns_of(1, 0))
    spread_1 = summed(1, reduce_1)
    store_plane(2, columns_of(1, 1))
    last = columns_of(1, 2)
    back.wait_recv()
    edge = jnp.where(depth < 7, upper[...].astype(F32), 0.0)
    store_plane(3, last, [edge[:, phase_cells(phase)] for phase in range(4)])
    finish(0, zl, spread_0)
    finish(1, 1 - zl, spread_1)
    for copy in sent:
        copy.wait_send()


def on_device(volume, kernel, cotangent):
    planes = volume.transpose(1, 0, 2)
    upstream = cotangent.transpose(1, 0, 2)
    vmem = pl.BlockSpec(memory_space=pltpu.VMEM)
    scratch = [
        ((INS, 4 * CELLS), BF),
        ((INS, 4 * CELLS), BF),
        ((2 * LEVEL + DEEP, CELLS), BF),
        ((ALL, DEEP), BF),
        ((2, HALF, DEEP), BF),
        ((2, HALF, CELLS), BF),
        ((2, HALF, CELLS), BF),
        ((2, HALF, CELLS), F32),
        ((2, HALF, CELLS), BF),
        ((2, 7, OUTS, CELLS), BF),
        ((2, ALL, CELLS), BF),
        ((INS, 4 * CELLS), BF),
        ((2, 2, 4 * PIECE, PART), F32),
        ((2, 2, 4 * PIECE, PART), BF),
        ((2, 7, PIECE, PART), BF),
        ((2, 4, 2, PIECE, PART), BF),
    ]
    activated, grad_volume, grad_kernel = pl.pallas_call(
        body,
        out_shape=(
            jax.ShapeDtypeStruct((2, OUTS, CELLS), BF),
            jax.ShapeDtypeStruct((4, INS, 4 * CELLS), BF),
            jax.ShapeDtypeStruct((ROWS, ALL), F32),
        ),
        in_specs=[vmem] * 3,
        out_specs=(vmem,) * 3,
        scratch_shapes=[pltpu.VMEM(shape, kind) for shape, kind in scratch]
        + [pltpu.SemaphoreType.DMA((COPIES,)), pltpu.SemaphoreType.DMA((COPIES,))],
        compiler_params=pltpu.CompilerParams(
            collective_id=0, has_side_effects=True, vmem_limit_bytes=48 * 1024 * 1024
        ),
    )(planes, kernel.reshape(ROWS, ALL), upstream)
    return (
        activated.transpose(1, 0, 2),
        grad_volume.transpose(1, 0, 2),
        grad_kernel.reshape(TAPS, INS, ALL),
    )


def solution(mesh):
    return jax.shard_map(
        on_device,
        mesh=mesh,
        in_specs=(P("chan", "depth", None), P(None, "chan", None), P("chan", "depth", None)),
        out_specs=(P("chan", "depth", None), P("chan", "depth", None), P(None, "chan", None)),
        check_vma=False,
    )
```

time: 73.1 us -> 60.8 us (0.83)
  the two profiles are of different devices: /device:TPU:4 before, /device:TPU:22 now
where the time goes in v1:
time: 60.8 us; the launch traced here: 60.6 us
  Pallas kernels  54.7 us (90%)
  local copies, waits for them, and re-layouts  5.23 us (9%)
  between operations  0.66 us (1%)
    pallas_call x1, Pallas kernels, on_device(): pl.pallas_call(body, out_shape=(jax.ShapeDtypeStruct((2, OUTS, CELLS), BF...  54.7 us
    unnamed x7, local copies, waits for them, and re-layouts  5.23 us

profile of v1, /device:TPU:22, one launch (start us, length us, event | category | flops | bytes accessed | tf_op | source)
XLA Modules:
  0.0 60.6 jit_solution(7366938957920323199)
XLA Ops:
  0.6 0.9 %copy.13 = bf16[32,2,1024]{2,0,1:T(8,128)(2,1)S(1)} copy(bf16[32,2,1024]{2,1,0:T(2,128)(2,1)} %param.5) | data formatting | bytes 262144 | tf_op args[2]
  1.6 0.0 copy-start
  1.6 1.4 %copy.12 = bf16[16,4,4096]{2,0,1:T(8,128)(2,1)S(1)} copy(bf16[16,4,4096]{2,1,0:T(4,128)(2,1)} %param.3) | data formatting | bytes 1048576 | tf_op args[0]
  3.0 0.0 copy-done
  3.0 54.7 %shard_map.58 = (bf16[2,32,1024]{2,1,0:T(8,128)(2,1)S(1)}, bf16[4,16,4096]{2,1,0:T(8,128)(2,1)S(1)}, f32[432,512]{1,0:T(8,128)S(1)}) custom-call(bf16[4,16,4096]{2,1,0:T(8,128)(2,1)S(1)} %bitcast.10, bf16[432,512]{1,0:T(8,128)(2,1)S(1)} %bitcast.14, bf16[2,32,1024]{2,1,0:T(8,128)(2,1)S(1)} %bitcast.12), custom_call_target="tpu_custom_call" | custom-call | tf_op jit(solution)/shard_map/pallas_call | solution.py:300
  57.7 0.8 %copy.8 = bf16[32,2,1024]{2,1,0:T(2,128)(2,1)} copy(bf16[32,2,1024]{2,0,1:T(8,128)(2,1)S(1)} %bitcast.15) | data formatting | bytes 262144
  58.5 1.2 %copy.9 = bf16[16,4,4096]{2,1,0:T(4,128)(2,1)} copy(bf16[16,4,4096]{2,0,1:T(8,128)(2,1)S(1)} %bitcast.13) | data formatting | bytes 1048576
  59.7 0.9 %copy.15 = f32[27,16,512]{2,1,0:T(8,128)} copy(f32[27,16,512]{2,1,0:T(8,128)S(1)} %bitcast.11) | data formatting | bytes 1769472
Async XLA Ops:
  1.6 1.4 %copy-start = (bf16[27,16,512]{2,1,0:T(8,128)(2,1)S(1)}, bf16[27,16,512]{2,1,0:T(8,128)(2,1)}, u32[]{:S(2)}) copy-start(bf16[27,16,512]{2,1,0:T(8,128)(2,1)} %param.4) | copy-start | bytes 1327108

commit v2 on v1

--- a/solution.py
+++ b/solution.py
@@ -52,13 +52,42 @@
     return keep
 
 
+def unpack(src, rows):
+    count, group, width = src.shape
+    for tile in range(width // 128):
+        size = count * group
+        block = src[:, :, tile * 128 : tile * 128 + 128].astype(F32)
+        rows[tile * size : tile * size + size, :] = block.reshape(size, 128)
+
+
+def take(rows, count, group, place):
+    size = count * group
+    tiles = [rows[pl.ds(tile * size + place, count, stride=group), :] for tile in range(rows.shape[0] // size)]
+    return jnp.concatenate(tiles, axis=1)
+
+
+def put(rows, count, group, place, first, value):
+    size = count * group
+    for tile in range(value.shape[1] // 128):
+        start = (first + tile) * size + place
+        rows[pl.ds(start, count, stride=group), :] = value[:, tile * 128 : tile * 128 + 128]
+
+
+def pack(rows, dst):
+    count, group, width = dst.shape
+    for tile in range(width // 128):
+        size = count * group
+        block = rows[tile * size : tile * size + size, :].reshape(count, group, 128)
+        dst[:, :, tile * 128 : tile * 128 + 128] = block.astype(BF)
+
+
 def dot(left, right, contract):
     return lax.dot_general(left, right, (contract, ((), ())), preferred_element_type=F32)
 
 
 def body(
     vol, wk, cot, act, gvol, gker,
-    low, upper, views, wfull, wt, sib_out, sib_in, acc, rs_out, rs_in,
+    low, upper, top, vol_rows, cot_rows, act_rows, gvol_rows, views, wt, sib_out, sib_in, acc, rs_out, rs_in,
     grads, back_out, filt, filt_out, filt_in, gk16,
     send_sem, recv_sem,
 ):
@@ -98,8 +127,7 @@
         sent.append(copy)
         return copy
 
-    def build(level, plane):
-        wide = plane.astype(F32)
+    def build(level, wide):
         for tap, phase, row_step, col_step in taps_2d():
             view = wide[:, phase * CELLS : (phase + 1) * CELLS]
             amount = -row_step * SIDE - col_step
@@ -108,23 +136,27 @@
             start = level * LEVEL + tap * INS
             views[start : start + INS, :] = view.astype(BF)
 
-    wfull[0:ROWS, :] = wk[...]
-    wfull[ROWS:DEEP, :] = jnp.zeros((DEEP - ROWS, ALL), BF)
-    wfull[...] = wfull[...].T
+    unpack(vol, vol_rows)
+
+    def plane(p):
+        return take(vol_rows, INS, 4, p)
+
+    top[...] = plane(3).astype(BF)
+    pl.semaphore_wait(barrier, len(peers))
+    halo = push(top, low, above)
+
+    views[5 * LEVEL :, :] = jnp.zeros((views.shape[0] - 5 * LEVEL, CELLS), BF)
+    for p in (1, 2, 3):
+        build(p + 1, plane(p))
+
     for other in range(2):
-        for z_rel in range(2):
-            for x_rel in range(4):
-                block = ((zl + z_rel) % 2) * 8 + ((x + x_rel) % 4) * 2 + (core + other) % 2
-                rows = pl.ds(pl.multiple_of(block * OUTS, OUTS), OUTS)
-                start = (z_rel * 4 + x_rel) * OUTS
-                wt[other, start : start + OUTS, :] = wfull[rows, :]
-
-    pl.semaphore_wait(barrier, len(peers))
-    halo = push(vol.at[3], low, above)
-
-    views[5 * LEVEL :, :] = jnp.zeros((views.shape[0] - 5 * LEVEL, CELLS), BF)
-    for plane in (1, 2, 3):
-        build(plane + 1, vol[plane])
+        row = lax.broadcasted_iota(jnp.int32, (HALF, ALL), 0)
+        channel = lax.broadcasted_iota(jnp.int32, (HALF, ALL), 1)
+        z_rel, x_rel, within = row // (4 * OUTS), (row // OUTS) % 4, row % OUTS
+        wanted = ((zl + z_rel) % 2) * HALF + ((x + x_rel) % 4) * (2 * OUTS) + ((core + other) % 2) * OUTS + within
+        select = jnp.where(channel == wanted, 1.0, 0.0).astype(BF)
+        wt[other, :, 0:ROWS] = dot(select, wk[...], ((1,), (1,))).astype(BF)
+        wt[other, :, ROWS:DEEP] = jnp.zeros((HALF, DEEP - ROWS), BF)
 
     def partial(q, other):
         first = 2 * LEVEL * q
@@ -147,9 +179,10 @@
     sib_1 = to_sibling(1)
     acc[1] = partial(1, 0)
     scatter_1 = scatter(1, sib_1)
-    build(1, vol[0])
+    unpack(cot, cot_rows)
+    build(1, plane(0))
     halo.wait_recv()
-    build(0, jnp.where(depth > 0, low[...], jnp.zeros((), BF)))
+    build(0, jnp.where(depth > 0, low[...].astype(F32), 0.0))
     sib_0 = to_sibling(0)
     acc[0] = partial(0, 0)
     scatter_0 = scatter(0, sib_0)
@@ -164,33 +197,46 @@
         for n in range(len(moves)):
             preact = preact + rs_in[q, n].astype(F32)
         s = 1.0 / (1.0 + jnp.exp(-preact))
-        act[q] = (preact * s).astype(BF)
-        grad = cot[q].astype(F32) * s * (1.0 + preact * (1.0 - s))
+        put(act_rows, OUTS, 2, q, 0, preact * s)
+        grad = take(cot_rows, OUTS, 2, q) * s * (1.0 + preact * (1.0 - s))
         grads[q, pl.ds(rows_abs(0, 0), OUTS), :] = grad.astype(BF)
 
     def spread(q, start, target):
         place = grads.at[q, pl.ds(start, OUTS), :]
         return push(place, place, target)
 
-    def gather(q):
-        copies = {move: spread(q, rows_abs(0, 0), at_chan(*move)) for move in moves}
-        return copies, {(0, 0): spread(q, rows_abs(0, 0), sibling)}
-
-    def share(q, gathered, group):
-        for dz, dx in group:
-            gathered[0][dz, dx].wait_recv()
-            gathered[1][dz, dx] = spread(q, rows_abs(dz, -dx), sibling)
-
+    shared = {0: {}, 1: {}}
+
+    def share(q, move):
+        dz, dx = move
+        shared[q][move] = spread(q, rows_abs(dz, -dx), sibling)
+
+    pair = at_chan(1, 0)
+    across = {}
     activate(1, scatter_1)
-    gathered_1 = gather(1)
+    near_1 = {move: spread(1, rows_abs(0, 0), at_chan(*move)) for move in near}
+    across[1, 0] = spread(1, rows_abs(0, 0), pair)
+    share(1, (0, 0))
     activate(0, scatter_0)
-    gathered_0 = gather(0)
-    share(1, gathered_1, near)
-    share(1, gathered_1, far)
-    share(0, gathered_0, near)
-    for gathered in (gathered_1, gathered_0):
+    across_0 = spread(0, rows_abs(0, 0), pair)
+    near_0 = {move: spread(0, rows_abs(0, 0), at_chan(*move)) for move in near}
+    share(0, (0, 0))
+    for move in near:
+        near_1[move].wait_recv()
+        across[1, move[1]] = spread(1, rows_abs(0, -move[1]), pair)
+        share(1, move)
+    across_0.wait_recv()
+    far_0 = {(1, dx): spread(0, rows_abs(1, 0), at_chan(0, dx)) for _, dx in near}
+    share(0, (1, 0))
+    across[1, 0].wait_recv()
+    share(1, (1, 0))
+    for move in near:
+        near_0[move].wait_recv()
+        share(0, move)
+    for q in range(2):
         for move in [(0, 0)] + near:
-            gathered[1][move].wait_recv()
+            shared[q][move].wait_recv()
+    pack(act_rows, act)
 
     def filters(part, z):
         columns = pl.ds(pl.multiple_of(z * HALF, HALF), HALF)
@@ -202,7 +248,7 @@
         filt[part, :, ROWS:, :] = jnp.zeros((2, 4 * PIECE - ROWS, PART), F32)
         filt_out[part] = filt[part].astype(BF)
         copies = []
-        for n, (dz, dy) in enumerate(moves):
+        for n, (dz, dy) in enumerate(far + near):
             start = pl.multiple_of(((y + dy) % 4) * PIECE, PIECE)
             src = filt_out.at[part, (zh + dz) % 2, pl.ds(start, PIECE), :]
             copies.append(push(src, filt_in.at[part, n], at_depth(dz, dy)))
@@ -217,7 +263,7 @@
             total = total + filt_in[part, n].astype(F32)
         gk16[part, y, zh] = total.astype(BF)
         place = gk16.at[part, y, zh]
-        return [push(place, place, at_depth(*move)) for move in moves]
+        return [push(place, place, at_depth(*move)) for move in far + near]
 
     def finish(part, z, copies):
         for copy in copies:
@@ -229,10 +275,14 @@
                 gker[y_ * PIECE : y_ * PIECE + rows, columns] = gk16[part, y_, side, :rows, :].astype(F32)
 
     reduce_0 = filters(0, zl)
-    share(0, gathered_0, far)
-    for gathered in (gathered_1, gathered_0):
+    for _, dx in near:
+        across[1, dx].wait_recv()
+        share(1, (1, dx))
+        far_0[1, dx].wait_recv()
+        share(0, (1, dx))
+    for q in range(2):
         for move in far:
-            gathered[1][move].wait_recv()
+            shared[q][move].wait_recv()
     reduce_1 = filters(1, 1 - zl)
 
     def spatial(columns):
@@ -254,7 +304,7 @@
     def store_plane(plane, parts, more=None):
         for phase in range(4):
             total = parts[phase] if more is None else parts[phase] + more[phase]
-            gvol[plane, :, phase_cells(phase)] = total.astype(BF)
+            put(gvol_rows, INS, 4, plane, phase * (CELLS // 128), total)
 
     lowest = columns_of(0, 0)
     for phase in range(4):
@@ -269,21 +319,36 @@
     back.wait_recv()
     edge = jnp.where(depth < 7, upper[...].astype(F32), 0.0)
     store_plane(3, last, [edge[:, phase_cells(phase)] for phase in range(4)])
+    pack(gvol_rows, gvol)
     finish(0, zl, spread_0)
     finish(1, 1 - zl, spread_1)
     for copy in sent:
         copy.wait_send()
 
 
+def store(act, gvol, gker, act_out, gvol_out, gker_out, sems):
+    parts = [(act, act_out), (gvol.at[0:8], gvol_out.at[0:8]), (gvol.at[8:16], gvol_out.at[8:16])]
+    for first in range(0, ROWS, LEVEL):
+        rows = slice(first, first + LEVEL)
+        parts.append((gker.at[rows, :], gker_out.at[rows, :]))
+    copies = [pltpu.make_async_copy(src, dst, sems.at[n]) for n, (src, dst) in enumerate(parts)]
+    for copy in copies:
+        copy.start()
+    for copy in copies:
+        copy.wait()
+
+
 def on_device(volume, kernel, cotangent):
-    planes = volume.transpose(1, 0, 2)
-    upstream = cotangent.transpose(1, 0, 2)
     vmem = pl.BlockSpec(memory_space=pltpu.VMEM)
     scratch = [
         ((INS, 4 * CELLS), BF),
         ((INS, 4 * CELLS), BF),
+        ((INS, 4 * CELLS), BF),
+        ((4 * INS * CELLS // 32, 128), F32),
+        ((2 * OUTS * CELLS // 128, 128), F32),
+        ((2 * OUTS * CELLS // 128, 128), F32),
+        ((4 * INS * CELLS // 32, 128), F32),
         ((2 * LEVEL + DEEP, CELLS), BF),
-        ((ALL, DEEP), BF),
         ((2, HALF, DEEP), BF),
         ((2, HALF, CELLS), BF),
         ((2, HALF, CELLS), BF),
@@ -300,8 +365,8 @@
     activated, grad_volume, grad_kernel = pl.pallas_call(
         body,
         out_shape=(
-            jax.ShapeDtypeStruct((2, OUTS, CELLS), BF),
-            jax.ShapeDtypeStruct((4, INS, 4 * CELLS), BF),
+            jax.ShapeDtypeStruct(cotangent.shape, BF),
+            jax.ShapeDtypeStruct(volume.shape, BF),
             jax.ShapeDtypeStruct((ROWS, ALL), F32),
         ),
         in_specs=[vmem] * 3,
@@ -311,12 +376,17 @@
         compiler_params=pltpu.CompilerParams(
             collective_id=0, has_side_effects=True, vmem_limit_bytes=48 * 1024 * 1024
         ),
-    )(planes, kernel.reshape(ROWS, ALL), upstream)
-    return (
-        activated.transpose(1, 0, 2),
-        grad_volume.transpose(1, 0, 2),
-        grad_kernel.reshape(TAPS, INS, ALL),
-    )
+    )(volume, kernel.reshape(ROWS, ALL), cotangent)
+    whole = pl.BlockSpec(memory_space=pl.ANY)
+    results = (activated, grad_volume, grad_kernel)
+    activated, grad_volume, grad_kernel = pl.pallas_call(
+        store,
+        out_shape=tuple(jax.ShapeDtypeStruct(r.shape, r.dtype) for r in results),
+        in_specs=[vmem] * 3,
+        out_specs=(whole,) * 3,
+        scratch_shapes=[pltpu.SemaphoreType.DMA((6,))],
+    )(*results)
+    return activated, grad_volume, grad_kernel.reshape(TAPS, INS, ALL)
 
 
 def solution(mesh):

time: 60.8 us -> 60.4 us (level)
  the two profiles are of different devices: /device:TPU:22 before, /device:TPU:1 now
where the time goes in v2:
time: 60.4 us; the launch traced here: 59.5 us
  Pallas kernels  53.5 us (89%)
  local copies, waits for them, and re-layouts  5.32 us (9%)
  between operations  0.66 us (1%)
    pallas_call x1, Pallas kernels, on_device(): pl.pallas_call(body, out_shape=(jax.ShapeDtypeStruct(cotangent.shape, BF)...  51 us
    unnamed x12, local copies, waits for them, and re-layouts  5.32 us
    pallas_call x1, Pallas kernels, on_device(): pl.pallas_call(store, out_shape=tuple((jax.ShapeDtypeStruct(r.shape, r.dt...  2.54 us

profile of v2, /device:TPU:1, one launch (start us, length us, event | category | flops | bytes accessed | tf_op | source)
XLA Modules:
  0.0 59.5 jit_solution(15716956155252981645)
XLA Ops:
  0.6 0.0 copy-start.2
  0.6 1.0 %copy-done.2 = bf16[16,4,4096]{2,1,0:T(4,128)(2,1)S(1)} copy-done((bf16[16,4,4096]{2,1,0:T(4,128)(2,1)S(1)}, bf16[16,4,4096]{2,1,0:T(4,128)(2,1)}, u32[]{:S(2)}) %copy-start.2) | copy-done | bytes 524312
  1.7 0.0 copy-start.3
  1.7 1.0 %copy-done.3 = bf16[27,16,512]{2,1,0:T(8,128)(2,1)S(1)} copy-done((bf16[27,16,512]{2,1,0:T(8,128)(2,1)S(1)}, bf16[27,16,512]{2,1,0:T(8,128)(2,1)}, u32[]{:S(2)}) %copy-start.3) | copy-done | bytes 442392
  2.7 0.0 copy-start.4
  2.7 0.9 %copy-done.4 = bf16[32,2,1024]{2,1,0:T(2,128)(2,1)S(1)} copy-done((bf16[32,2,1024]{2,1,0:T(2,128)(2,1)S(1)}, bf16[32,2,1024]{2,1,0:T(2,128)(2,1)}, u32[]{:S(2)}) %copy-start.4) | copy-done | bytes 131096
  3.6 51.0 %shard_map.58 = (bf16[32,2,1024]{2,1,0:T(2,128)(2,1)S(1)}, bf16[16,4,4096]{2,1,0:T(4,128)(2,1)S(1)}, f32[432,512]{1,0:T(8,128)S(1)}) custom-call(bf16[16,4,4096]{2,1,0:T(4,128)(2,1)S(1)} %copy-done.2, bf16[432,512]{1,0:T(8,128)(2,1)S(1)} %bitcast.2, bf16[32,2,1024]{2,1,0:T(2,128)(2,1)S(1)} %copy-done.4), custom_call_target="tpu_custom_call" | custom-call | tf_op jit(solution)/shard_map/pallas_call | solution.py:365
  54.6 0.0 copy-start
  54.6 0.9 %copy-done = f32[432,512]{1,0:T(8,128)} copy-done((f32[432,512]{1,0:T(8,128)}, f32[432,512]{1,0:T(8,128)S(1)}, u32[]{:S(2)}) %copy-start) | copy-done | bytes 884760
  55.5 0.0 copy-start.1
  55.5 0.8 %copy-done.1 = bf16[16,4,4096]{2,1,0:T(4,128)(2,1)} copy-done((bf16[16,4,4096]{2,1,0:T(4,128)(2,1)}, bf16[16,4,4096]{2,1,0:T(4,128)(2,1)S(1)}, u32[]{:S(2)}) %copy-start.1) | copy-done | bytes 524312
  56.3 0.0 copy-start.5
  56.3 0.6 %copy-done.5 = bf16[32,2,1024]{2,1,0:T(2,128)(2,1)} copy-done((bf16[32,2,1024]{2,1,0:T(2,128)(2,1)}, bf16[32,2,1024]{2,1,0:T(2,128)(2,1)S(1)}, u32[]{:S(2)}) %copy-start.5) | copy-done | bytes 131096
  57.0 2.5 %shard_map.59 = (bf16[32,2,1024]{2,1,0:T(2,128)(2,1)}, bf16[16,4,4096]{2,1,0:T(4,128)(2,1)}, f32[432,512]{1,0:T(8,128)}) custom-call(bf16[32,2,1024]{2,1,0:T(2,128)(2,1)} %copy-done.5, bf16[16,4,4096]{2,1,0:T(4,128)(2,1)} %copy-done.1, f32[432,512]{1,0:T(8,128)} %copy-done), custom_call_target="tpu_custom_call" | custom-call | tf_op jit(solution)/shard_map/pallas_call | solution.py:382
Async XLA Ops:
  0.6 1.0 %copy-start.2 = (bf16[16,4,4096]{2,1,0:T(4,128)(2,1)S(1)}, bf16[16,4,4096]{2,1,0:T(4,128)(2,1)}, u32[]{:S(2)}) copy-start(bf16[16,4,4096]{2,1,0:T(4,128)(2,1)} %vol.1) | copy-start | bytes 1572868
  1.7 1.0 %copy-start.3 = (bf16[27,16,512]{2,1,0:T(8,128)(2,1)S(1)}, bf16[27,16,512]{2,1,0:T(8,128)(2,1)}, u32[]{:S(2)}) copy-start(bf16[27,16,512]{2,1,0:T(8,128)(2,1)} %param.4) | copy-start | bytes 1327108
  2.7 0.9 %copy-start.4 = (bf16[32,2,1024]{2,1,0:T(2,128)(2,1)S(1)}, bf16[32,2,1024]{2,1,0:T(2,128)(2,1)}, u32[]{:S(2)}) copy-start(bf16[32,2,1024]{2,1,0:T(2,128)(2,1)} %cot.1) | copy-start | bytes 393220
  54.6 0.9 %copy-start = (f32[432,512]{1,0:T(8,128)}, f32[432,512]{1,0:T(8,128)S(1)}, u32[]{:S(2)}) copy-start(f32[432,512]{1,0:T(8,128)S(1)} %get-tuple-element.11.gker) | copy-start | bytes 2654212
  55.5 0.8 %copy-start.1 = (bf16[16,4,4096]{2,1,0:T(4,128)(2,1)}, bf16[16,4,4096]{2,1,0:T(4,128)(2,1)S(1)}, u32[]{:S(2)}) copy-start(bf16[16,4,4096]{2,1,0:T(4,128)(2,1)S(1)} %get-tuple-element.10.gvol) | copy-start | bytes 1572868
  56.3 0.6 %copy-start.5 = (bf16[32,2,1024]{2,1,0:T(2,128)(2,1)}, bf16[32,2,1024]{2,1,0:T(2,128)(2,1)S(1)}, u32[]{:S(2)}) copy-start(bf16[32,2,1024]{2,1,0:T(2,128)(2,1)S(1)} %get-tuple-element.9.act) | copy-start | bytes 393220

commit v3 on v2

--- a/solution.py
+++ b/solution.py
@@ -86,11 +86,25 @@
 
 
 def body(
+    vol_hbm, wk_hbm, cot_hbm, act_hbm, gvol_hbm, gker_hbm,
     vol, wk, cot, act, gvol, gker,
     low, upper, top, vol_rows, cot_rows, act_rows, gvol_rows, views, wt, sib_out, sib_in, acc, rs_out, rs_in,
     grads, back_out, filt, filt_out, filt_in, gk16,
-    send_sem, recv_sem,
+    send_sem, recv_sem, load_sem, save_sem,
 ):
+    loads = [
+        pltpu.make_async_copy(src, dst, load_sem.at[n])
+        for n, (src, dst) in enumerate(((vol_hbm, vol), (wk_hbm, wk), (cot_hbm, cot)))
+    ]
+    for load in loads:
+        load.start()
+    saves = []
+
+    def save(src, dst):
+        copy = pltpu.make_async_copy(src, dst, save_sem.at[len(saves)])
+        copy.start()
+        saves.append(copy)
+
     depth = lax.axis_index("depth")
     chan = lax.axis_index("chan")
     y, zh = depth // 2, depth % 2
@@ -136,6 +150,7 @@
             start = level * LEVEL + tap * INS
             views[start : start + INS, :] = view.astype(BF)
 
+    loads[0].wait()
     unpack(vol, vol_rows)
 
     def plane(p):
@@ -149,6 +164,7 @@
     for p in (1, 2, 3):
         build(p + 1, plane(p))
 
+    loads[1].wait()
     for other in range(2):
         row = lax.broadcasted_iota(jnp.int32, (HALF, ALL), 0)
         channel = lax.broadcasted_iota(jnp.int32, (HALF, ALL), 1)
@@ -179,6 +195,7 @@
     sib_1 = to_sibling(1)
     acc[1] = partial(1, 0)
     scatter_1 = scatter(1, sib_1)
+    loads[2].wait()
     unpack(cot, cot_rows)
     build(1, plane(0))
     halo.wait_recv()
@@ -237,6 +254,7 @@
         for move in [(0, 0)] + near:
             shared[q][move].wait_recv()
     pack(act_rows, act)
+    save(act, act_hbm)
 
     def filters(part, z):
         columns = pl.ds(pl.multiple_of(z * HALF, HALF), HALF)
@@ -273,6 +291,8 @@
             for side in range(2):
                 columns = pl.ds(pl.multiple_of(z * HALF + side * PART, PART), PART)
                 gker[y_ * PIECE : y_ * PIECE + rows, columns] = gk16[part, y_, side, :rows, :].astype(F32)
+        columns = pl.ds(pl.multiple_of(z * HALF, HALF), HALF)
+        save(gker.at[:, columns], gker_hbm.at[:, columns])
 
     reduce_0 = filters(0, zl)
     for _, dx in near:
@@ -320,27 +340,42 @@
     edge = jnp.where(depth < 7, upper[...].astype(F32), 0.0)
     store_plane(3, last, [edge[:, phase_cells(phase)] for phase in range(4)])
     pack(gvol_rows, gvol)
+    save(gvol, gvol_hbm)
     finish(0, zl, spread_0)
     finish(1, 1 - zl, spread_1)
     for copy in sent:
         copy.wait_send()
-
-
-def store(act, gvol, gker, act_out, gvol_out, gker_out, sems):
-    parts = [(act, act_out), (gvol.at[0:8], gvol_out.at[0:8]), (gvol.at[8:16], gvol_out.at[8:16])]
+    for copy in saves:
+        copy.wait()
+
+
+def store(act, gvol, gker, act_out, gvol_out, gker_out, act_in, gvol_in, gker_in, load_sem, save_sem):
+    parts = [(act, act_in, act_out)]
+    for first in range(0, INS, 8):
+        rows = slice(first, first + 8)
+        parts.append((gvol.at[rows], gvol_in.at[rows], gvol_out.at[rows]))
     for first in range(0, ROWS, LEVEL):
         rows = slice(first, first + LEVEL)
-        parts.append((gker.at[rows, :], gker_out.at[rows, :]))
-    copies = [pltpu.make_async_copy(src, dst, sems.at[n]) for n, (src, dst) in enumerate(parts)]
-    for copy in copies:
-        copy.start()
-    for copy in copies:
-        copy.wait()
+        parts.append((gker.at[rows, :], gker_in.at[rows, :], gker_out.at[rows, :]))
+    loads = [pltpu.make_async_copy(src, mid, load_sem.at[n]) for n, (src, mid, _) in enumerate(parts)]
+    saves = [pltpu.make_async_copy(mid, dst, save_sem.at[n]) for n, (_, mid, dst) in enumerate(parts)]
+    for load in loads:
+        load.start()
+    for load, save in zip(loads, saves):
+        load.wait()
+        save.start()
+    for save in saves:
+        save.wait()
 
 
 def on_device(volume, kernel, cotangent):
-    vmem = pl.BlockSpec(memory_space=pltpu.VMEM)
     scratch = [
+        (volume.shape, BF),
+        ((ROWS, ALL), BF),
+        (cotangent.shape, BF),
+        (cotangent.shape, BF),
+        (volume.shape, BF),
+        ((ROWS, ALL), F32),
         ((INS, 4 * CELLS), BF),
         ((INS, 4 * CELLS), BF),
         ((INS, 4 * CELLS), BF),
@@ -362,6 +397,7 @@
         ((2, 7, PIECE, PART), BF),
         ((2, 4, 2, PIECE, PART), BF),
     ]
+    whole = pl.BlockSpec(memory_space=pl.ANY)
     activated, grad_volume, grad_kernel = pl.pallas_call(
         body,
         out_shape=(
@@ -369,22 +405,23 @@
             jax.ShapeDtypeStruct(volume.shape, BF),
             jax.ShapeDtypeStruct((ROWS, ALL), F32),
         ),
-        in_specs=[vmem] * 3,
-        out_specs=(vmem,) * 3,
+        in_specs=[whole] * 3,
+        out_specs=(whole,) * 3,
         scratch_shapes=[pltpu.VMEM(shape, kind) for shape, kind in scratch]
-        + [pltpu.SemaphoreType.DMA((COPIES,)), pltpu.SemaphoreType.DMA((COPIES,))],
+        + [pltpu.SemaphoreType.DMA((COPIES,)), pltpu.SemaphoreType.DMA((COPIES,)), pltpu.SemaphoreType.DMA((3,)), pltpu.SemaphoreType.DMA((4,))],
         compiler_params=pltpu.CompilerParams(
-            collective_id=0, has_side_effects=True, vmem_limit_bytes=48 * 1024 * 1024
+            collective_id=0, has_side_effects=True, vmem_limit_bytes=56 * 1024 * 1024
         ),
     )(volume, kernel.reshape(ROWS, ALL), cotangent)
-    whole = pl.BlockSpec(memory_space=pl.ANY)
     results = (activated, grad_volume, grad_kernel)
     activated, grad_volume, grad_kernel = pl.pallas_call(
         store,
         out_shape=tuple(jax.ShapeDtypeStruct(r.shape, r.dtype) for r in results),
-        in_specs=[vmem] * 3,
+        in_specs=[whole] * 3,
         out_specs=(whole,) * 3,
-        scratch_shapes=[pltpu.SemaphoreType.DMA((6,))],
+        scratch_shapes=[pltpu.VMEM(r.shape, r.dtype) for r in results]
+        + [pltpu.SemaphoreType.DMA((6,)), pltpu.SemaphoreType.DMA((6,))],
+        compiler_params=pltpu.CompilerParams(vmem_limit_bytes=56 * 1024 * 1024),
     )(*results)
     return activated, grad_volume, grad_kernel.reshape(TAPS, INS, ALL)
 

time: 60.4 us -> 57.8 us (0.957); the launches traced: 59.5 us -> 57.7 us
  local copies, waits for them, and re-layouts: 5.32 us -> 0 us
  Pallas kernels: 53.5 us -> 57.1 us
    unnamed x12 -> x0, local copies, waits for them, and re-layouts: 5.32 us -> none
    pallas_call x1, Pallas kernels: 51 us -> 54.8 us  [on_device(): pl.pallas_call(body, out_shape=(jax.ShapeDtypeStruct(cotangent.shape, BF)...]
where the time goes in v3:
time: 57.8 us; the launch traced here: 57.7 us
  Pallas kernels  57.1 us (99%)
  between operations  0.64 us (1%)
    pallas_call x1, Pallas kernels, on_device(): pl.pallas_call(body, out_shape=(jax.ShapeDtypeStruct(cotangent.shape, BF)...  54.8 us
    pallas_call x1, Pallas kernels, on_device(): pl.pallas_call(store, out_shape=tuple((jax.ShapeDtypeStruct(r.shape, r.dt...  2.21 us

profile of v3, /device:TPU:1, one launch (start us, length us, event | category | flops | bytes accessed | tf_op | source)
XLA Modules:
  0.0 57.7 jit_solution(14749892468826400764)
XLA Ops:
  0.6 54.8 %shard_map.58 = (bf16[32,2,1024]{2,1,0:T(2,128)(2,1)}, bf16[16,4,4096]{2,1,0:T(4,128)(2,1)}, f32[432,512]{1,0:T(8,128)}) custom-call(bf16[16,4,4096]{2,1,0:T(4,128)(2,1)} %vol_hbm.1, bf16[432,512]{1,0:T(8,128)(2,1)} %bitcast.2, bf16[32,2,1024]{2,1,0:T(2,128)(2,1)} %cot_hbm.1), custom_call_target="tpu_custom_call" | custom-call | tf_op jit(solution)/shard_map/pallas_call | solution.py:401
  55.5 2.2 %shard_map.59 = (bf16[32,2,1024]{2,1,0:T(2,128)(2,1)}, bf16[16,4,4096]{2,1,0:T(4,128)(2,1)}, f32[432,512]{1,0:T(8,128)}) custom-call(bf16[32,2,1024]{2,1,0:T(2,128)(2,1)} %get-tuple-element.9.act, bf16[16,4,4096]{2,1,0:T(4,128)(2,1)} %get-tuple-element.10.gvol, f32[432,512]{1,0:T(8,128)} %get-tuple-element.11.gker), custom_call_target="tpu_custom_call" | custom-call | tf_op jit(solution)/shard_map/pallas_call | solution.py:417

commit v4 on v3

--- a/solution.py
+++ b/solution.py
@@ -116,7 +116,7 @@
     def at_depth(dz, dy):
         return (((y + dy) % 4) * 2 + (zh + dz) % 2, chan)
 
-    near = [(0, 1), (0, 3), (0, 2)]
+    near = [(0, 2), (0, 1), (0, 3)]
     far = [(1, 0), (1, 1), (1, 3), (1, 2)]
     moves = near + far
     sibling = at_chan(0, 0, 1)
@@ -187,7 +187,7 @@
         acc[q] = acc[q] + sib_in[q].astype(F32)
         rs_out[q] = acc[q].astype(BF)
         copies = []
-        for n, (dz, dx) in enumerate(moves):
+        for n, (dz, dx) in enumerate(far + near):
             start = (dz * 4 + dx) * OUTS
             copies.append(push(rs_out.at[q, start : start + OUTS, :], rs_in.at[q, n], at_chan(dz, dx)))
         return copies
@@ -304,6 +304,7 @@
         for move in far:
             shared[q][move].wait_recv()
     reduce_1 = filters(1, 1 - zl)
+    spread_0 = summed(0, reduce_0)
 
     def spatial(columns):
         sums = {}
@@ -330,7 +331,6 @@
     for phase in range(4):
         back_out[:, phase_cells(phase)] = lowest[phase].astype(BF)
     back = push(back_out, upper, below)
-    spread_0 = summed(0, reduce_0)
     store_plane(0, columns_of(0, 1))
     store_plane(1, columns_of(0, 2), columns_of(1, 0))
     spread_1 = summed(1, reduce_1)

time: 57.8 us -> 54.2 us (0.938)
  Pallas kernels: 57.1 us -> 53.1 us
    pallas_call x1, Pallas kernels: 54.8 us -> 50.9 us  [on_device(): pl.pallas_call(body, out_shape=(jax.ShapeDtypeStruct(cotangent.shape, BF)...]
where the time goes in v4:
time: 54.2 us; the launch traced here: 53.8 us
  Pallas kernels  53.1 us (98%)
  between operations  0.64 us (1%)
    pallas_call x1, Pallas kernels, on_device(): pl.pallas_call(body, out_shape=(jax.ShapeDtypeStruct(cotangent.shape, BF)...  50.9 us
    pallas_call x1, Pallas kernels, on_device(): pl.pallas_call(store, out_shape=tuple((jax.ShapeDtypeStruct(r.shape, r.dt...  2.21 us

profile of v4, /device:TPU:1, one launch (start us, length us, event | category | flops | bytes accessed | tf_op | source)
XLA Modules:
  0.0 53.8 jit_solution(5222573557552962180)
XLA Ops:
  0.6 50.9 %shard_map.58 = (bf16[32,2,1024]{2,1,0:T(2,128)(2,1)}, bf16[16,4,4096]{2,1,0:T(4,128)(2,1)}, f32[432,512]{1,0:T(8,128)}) custom-call(bf16[16,4,4096]{2,1,0:T(4,128)(2,1)} %vol_hbm.1, bf16[432,512]{1,0:T(8,128)(2,1)} %bitcast.2, bf16[32,2,1024]{2,1,0:T(2,128)(2,1)} %cot_hbm.1), custom_call_target="tpu_custom_call" | custom-call | tf_op jit(solution)/shard_map/pallas_call | solution.py:401
  51.6 2.2 %shard_map.59 = (bf16[32,2,1024]{2,1,0:T(2,128)(2,1)}, bf16[16,4,4096]{2,1,0:T(4,128)(2,1)}, f32[432,512]{1,0:T(8,128)}) custom-call(bf16[32,2,1024]{2,1,0:T(2,128)(2,1)} %get-tuple-element.9.act, bf16[16,4,4096]{2,1,0:T(4,128)(2,1)} %get-tuple-element.10.gvol, f32[432,512]{1,0:T(8,128)} %get-tuple-element.11.gker), custom_call_target="tpu_custom_call" | custom-call | tf_op jit(solution)/shard_map/pallas_call | solution.py:417

commit v5 on v4

--- a/solution.py
+++ b/solution.py
@@ -87,9 +87,9 @@
 
 def body(
     vol_hbm, wk_hbm, cot_hbm, act_hbm, gvol_hbm, gker_hbm,
-    vol, wk, cot, act, gvol, gker,
+    vol, wk, cot, act, gvol,
     low, upper, top, vol_rows, cot_rows, act_rows, gvol_rows, views, wt, sib_out, sib_in, acc, rs_out, rs_in,
-    grads, back_out, filt, filt_out, filt_in, gk16,
+    grads, back_out, filt, filt_out, filt_in, final,
     send_sem, recv_sem, load_sem, save_sem,
 ):
     loads = [
@@ -120,6 +120,10 @@
     far = [(1, 0), (1, 1), (1, 3), (1, 2)]
     moves = near + far
     sibling = at_chan(0, 0, 1)
+
+    def by_core(first, second):
+        return [(a[0] + core * (b[0] - a[0]), a[1] + core * (b[1] - a[1])) for a, b in zip(first, second)]
+
     above = ((depth + 1) % 8, chan)
     below = ((depth + 7) % 8, chan)
 
@@ -187,9 +191,9 @@
         acc[q] = acc[q] + sib_in[q].astype(F32)
         rs_out[q] = acc[q].astype(BF)
         copies = []
-        for n, (dz, dx) in enumerate(far + near):
-            start = (dz * 4 + dx) * OUTS
-            copies.append(push(rs_out.at[q, start : start + OUTS, :], rs_in.at[q, n], at_chan(dz, dx)))
+        for n, (dz, dx) in enumerate(by_core(far + near, near + far)):
+            start = pl.multiple_of((dz * 4 + dx) * OUTS, OUTS)
+            copies.append(push(rs_out.at[q, pl.ds(start, OUTS), :], rs_in.at[q, n], at_chan(dz, dx)))
         return copies
 
     sib_1 = to_sibling(1)
@@ -272,27 +276,17 @@
             copies.append(push(src, filt_in.at[part, n], at_depth(dz, dy)))
         return copies
 
-    def summed(part, copies):
+    def summed(part, z, copies):
         for copy in copies:
             copy.wait_recv()
         start = pl.multiple_of(y * PIECE, PIECE)
         total = filt[part, zh, pl.ds(start, PIECE), :]
         for n in range(len(moves)):
             total = total + filt_in[part, n].astype(F32)
-        gk16[part, y, zh] = total.astype(BF)
-        place = gk16.at[part, y, zh]
-        return [push(place, place, at_depth(*move)) for move in far + near]
-
-    def finish(part, z, copies):
-        for copy in copies:
-            copy.wait_recv()
-        for y_ in range(4):
-            rows = min(PIECE, ROWS - y_ * PIECE)
-            for side in range(2):
-                columns = pl.ds(pl.multiple_of(z * HALF + side * PART, PART), PART)
-                gker[y_ * PIECE : y_ * PIECE + rows, columns] = gk16[part, y_, side, :rows, :].astype(F32)
-        columns = pl.ds(pl.multiple_of(z * HALF, HALF), HALF)
-        save(gker.at[:, columns], gker_hbm.at[:, columns])
+        final[part] = total.astype(BF)
+        place = gker_hbm.at[z, y, zh]
+        save(final.at[part], place)
+        return [push(final.at[part], place, at_depth(*move)) for move in far + near]
 
     reduce_0 = filters(0, zl)
     for _, dx in near:
@@ -304,7 +298,7 @@
         for move in far:
             shared[q][move].wait_recv()
     reduce_1 = filters(1, 1 - zl)
-    spread_0 = summed(0, reduce_0)
+    spread_0 = summed(0, zl, reduce_0)
 
     def spatial(columns):
         sums = {}
@@ -333,7 +327,7 @@
     back = push(back_out, upper, below)
     store_plane(0, columns_of(0, 1))
     store_plane(1, columns_of(0, 2), columns_of(1, 0))
-    spread_1 = summed(1, reduce_1)
+    spread_1 = summed(1, 1 - zl, reduce_1)
     store_plane(2, columns_of(1, 1))
     last = columns_of(1, 2)
     back.wait_recv()
@@ -341,31 +335,41 @@
     store_plane(3, last, [edge[:, phase_cells(phase)] for phase in range(4)])
     pack(gvol_rows, gvol)
     save(gvol, gvol_hbm)
-    finish(0, zl, spread_0)
-    finish(1, 1 - zl, spread_1)
+    for copy in spread_0 + spread_1:
+        copy.wait_recv()
     for copy in sent:
         copy.wait_send()
     for copy in saves:
         copy.wait()
 
 
-def store(act, gvol, gker, act_out, gvol_out, gker_out, act_in, gvol_in, gker_in, load_sem, save_sem):
-    parts = [(act, act_in, act_out)]
-    for first in range(0, INS, 8):
-        rows = slice(first, first + 8)
-        parts.append((gvol.at[rows], gvol_in.at[rows], gvol_out.at[rows]))
-    for first in range(0, ROWS, LEVEL):
-        rows = slice(first, first + LEVEL)
-        parts.append((gker.at[rows, :], gker_in.at[rows, :], gker_out.at[rows, :]))
-    loads = [pltpu.make_async_copy(src, mid, load_sem.at[n]) for n, (src, mid, _) in enumerate(parts)]
-    saves = [pltpu.make_async_copy(mid, dst, save_sem.at[n]) for n, (_, mid, dst) in enumerate(parts)]
-    for load in loads:
-        load.start()
-    for load, save in zip(loads, saves):
-        load.wait()
-        save.start()
-    for save in saves:
-        save.wait()
+def store(act, gvol, pieces, act_out, gvol_out, gker_out, act_in, gvol_in, pieces_in, gker, load_sem, save_sem):
+    loads, saves = [], []
+
+    def carry(src, dst, sems, copies):
+        copy = pltpu.make_async_copy(src, dst, sems.at[len(copies)])
+        copy.start()
+        copies.append(copy)
+
+    for z in range(2):
+        carry(pieces.at[z], pieces_in.at[z], load_sem, loads)
+    carry(gvol, gvol_in, load_sem, loads)
+    carry(act, act_in, load_sem, loads)
+    for z in range(2):
+        loads[z].wait()
+        for y in range(4):
+            rows = min(PIECE, ROWS - y * PIECE)
+            for side in range(2):
+                first = z * HALF + side * PART
+                gker[y * PIECE : y * PIECE + rows, first : first + PART] = pieces_in[z, y, side, :rows, :].astype(F32)
+        columns = slice(z * HALF, (z + 1) * HALF)
+        carry(gker.at[:, columns], gker_out.at[:, columns], save_sem, saves)
+    loads[2].wait()
+    carry(gvol_in, gvol_out, save_sem, saves)
+    loads[3].wait()
+    carry(act_in, act_out, save_sem, saves)
+    for copy in saves:
+        copy.wait()
 
 
 def on_device(volume, kernel, cotangent):
@@ -375,7 +379,6 @@
         (cotangent.shape, BF),
         (cotangent.shape, BF),
         (volume.shape, BF),
-        ((ROWS, ALL), F32),
         ((INS, 4 * CELLS), BF),
         ((INS, 4 * CELLS), BF),
         ((INS, 4 * CELLS), BF),
@@ -395,7 +398,7 @@
         ((2, 2, 4 * PIECE, PART), F32),
         ((2, 2, 4 * PIECE, PART), BF),
         ((2, 7, PIECE, PART), BF),
-        ((2, 4, 2, PIECE, PART), BF),
+        ((2, PIECE, PART), BF),
     ]
     whole = pl.BlockSpec(memory_space=pl.ANY)
     activated, grad_volume, grad_kernel = pl.pallas_call(
@@ -403,7 +406,7 @@
         out_shape=(
             jax.ShapeDtypeStruct(cotangent.shape, BF),
             jax.ShapeDtypeStruct(volume.shape, BF),
-            jax.ShapeDtypeStruct((ROWS, ALL), F32),
+            jax.ShapeDtypeStruct((2, 4, 2, PIECE, PART), BF),
         ),
         in_specs=[whole] * 3,
         out_specs=(whole,) * 3,
@@ -416,11 +419,15 @@
     results = (activated, grad_volume, grad_kernel)
     activated, grad_volume, grad_kernel = pl.pallas_call(
         store,
-        out_shape=tuple(jax.ShapeDtypeStruct(r.shape, r.dtype) for r in results),
+        out_shape=(
+            jax.ShapeDtypeStruct(cotangent.shape, BF),
+            jax.ShapeDtypeStruct(volume.shape, BF),
+            jax.ShapeDtypeStruct((ROWS, ALL), F32),
+        ),
         in_specs=[whole] * 3,
         out_specs=(whole,) * 3,
         scratch_shapes=[pltpu.VMEM(r.shape, r.dtype) for r in results]
-        + [pltpu.SemaphoreType.DMA((6,)), pltpu.SemaphoreType.DMA((6,))],
+        + [pltpu.VMEM((ROWS, ALL), F32), pltpu.SemaphoreType.DMA((4,)), pltpu.SemaphoreType.DMA((4,))],
         compiler_params=pltpu.CompilerParams(vmem_limit_bytes=56 * 1024 * 1024),
     )(*results)
     return activated, grad_volume, grad_kernel.reshape(TAPS, INS, ALL)

time: 54.2 us -> 53.3 us (0.983)
  Pallas kernels: 53.1 us -> 52.5 us
    pallas_call x1, Pallas kernels: 50.9 us -> 50.3 us  [on_device(): pl.pallas_call(body, out_shape=(jax.ShapeDtypeStruct(cotangent.shape, BF)...]
where the time goes in v5:
time: 53.3 us; the launch traced here: 53.1 us
  Pallas kernels  52.5 us (98%)
  between operations  0.64 us (1%)
    pallas_call x1, Pallas kernels, on_device(): pl.pallas_call(body, out_shape=(jax.ShapeDtypeStruct(cotangent.shape, BF)...  50.3 us
    pallas_call x1, Pallas kernels, on_device(): pl.pallas_call(store, out_shape=(jax.ShapeDtypeStruct(cotangent.shape, BF...  2.17 us

profile of v5, /device:TPU:1, one launch (start us, length us, event | category | flops | bytes accessed | tf_op | source)
XLA Modules:
  0.0 53.1 jit_solution(9575289905708869191)
XLA Ops:
  0.6 50.3 %shard_map.58 = (bf16[32,2,1024]{2,1,0:T(2,128)(2,1)}, bf16[16,4,4096]{2,1,0:T(4,128)(2,1)}, bf16[2,4,2,112,128]{4,3,2,1,0:T(8,128)(2,1)}) custom-call(bf16[16,4,4096]{2,1,0:T(4,128)(2,1)} %vol_hbm.1, bf16[432,512]{1,0:T(8,128)(2,1)} %bitcast.2, bf16[32,2,1024]{2,1,0:T(2,128)(2,1)} %cot_hbm.1), custom_call_target="tpu_custom_call" | custom-call | tf_op jit(solution)/shard_map/pallas_call | solution.py:404
  51.0 2.2 %shard_map.59 = (bf16[32,2,1024]{2,1,0:T(2,128)(2,1)}, bf16[16,4,4096]{2,1,0:T(4,128)(2,1)}, f32[432,512]{1,0:T(8,128)}) custom-call(bf16[32,2,1024]{2,1,0:T(2,128)(2,1)} %get-tuple-element.9.act, bf16[16,4,4096]{2,1,0:T(4,128)(2,1)} %get-tuple-element.10.gvol, bf16[2,4,2,112,128]{4,3,2,1,0:T(8,128)(2,1)} %get-tuple-element.11.pieces), custom_call_target="tpu_custom_call" | custom-call | tf_op jit(solution)/shard_map/pallas_call | solution.py:420

commit v6 on v5

--- a/solution.py
+++ b/solution.py
@@ -119,6 +119,7 @@
     near = [(0, 2), (0, 1), (0, 3)]
     far = [(1, 0), (1, 1), (1, 3), (1, 2)]
     moves = near + far
+    deep = [(1, 2), (1, 1), (1, 3), (1, 0)]
     sibling = at_chan(0, 0, 1)
 
     def by_core(first, second):
@@ -270,7 +271,7 @@
         filt[part, :, ROWS:, :] = jnp.zeros((2, 4 * PIECE - ROWS, PART), F32)
         filt_out[part] = filt[part].astype(BF)
         copies = []
-        for n, (dz, dy) in enumerate(far + near):
+        for n, (dz, dy) in enumerate(deep + near):
             start = pl.multiple_of(((y + dy) % 4) * PIECE, PIECE)
             src = filt_out.at[part, (zh + dz) % 2, pl.ds(start, PIECE), :]
             copies.append(push(src, filt_in.at[part, n], at_depth(dz, dy)))
@@ -286,7 +287,7 @@
         final[part] = total.astype(BF)
         place = gker_hbm.at[z, y, zh]
         save(final.at[part], place)
-        return [push(final.at[part], place, at_depth(*move)) for move in far + near]
+        return [push(final.at[part], place, at_depth(*move)) for move in by_core(far + near, near + far)]
 
     reduce_0 = filters(0, zl)
     for _, dx in near:
@@ -382,10 +383,10 @@
         ((INS, 4 * CELLS), BF),
         ((INS, 4 * CELLS), BF),
         ((INS, 4 * CELLS), BF),
-        ((4 * INS * CELLS // 32, 128), F32),
-        ((2 * OUTS * CELLS // 128, 128), F32),
-        ((2 * OUTS * CELLS // 128, 128), F32),
-        ((4 * INS * CELLS // 32, 128), F32),
+        ((4 * INS * CELLS // 32 + 8, 128), F32),
+        ((2 * OUTS * CELLS // 128 + 8, 128), F32),
+        ((2 * OUTS * CELLS // 128 + 8, 128), F32),
+        ((4 * INS * CELLS // 32 + 8, 128), F32),
         ((2 * LEVEL + DEEP, CELLS), BF),
         ((2, HALF, DEEP), BF),
         ((2, HALF, CELLS), BF),

time: 53.3 us -> 52.8 us (level)
  Pallas kernels: 52.5 us -> 51.5 us
    pallas_call x1, Pallas kernels: 50.3 us -> 49.3 us  [on_device(): pl.pallas_call(body, out_shape=(jax.ShapeDtypeStruct(cotangent.shape, BF)...]
where the time goes in v6:
time: 52.8 us; the launch traced here: 52.2 us
  Pallas kernels  51.5 us (98%)
  between operations  0.64 us (1%)
    pallas_call x1, Pallas kernels, on_device(): pl.pallas_call(body, out_shape=(jax.ShapeDtypeStruct(cotangent.shape, BF)...  49.3 us
    pallas_call x1, Pallas kernels, on_device(): pl.pallas_call(store, out_shape=(jax.ShapeDtypeStruct(cotangent.shape, BF...  2.17 us

profile of v6, /device:TPU:1, one launch (start us, length us, event | category | flops | bytes accessed | tf_op | source)
XLA Modules:
  0.0 52.2 jit_solution(11363553286454213028)
XLA Ops:
  0.6 49.3 %shard_map.58 = (bf16[32,2,1024]{2,1,0:T(2,128)(2,1)}, bf16[16,4,4096]{2,1,0:T(4,128)(2,1)}, bf16[2,4,2,112,128]{4,3,2,1,0:T(8,128)(2,1)}) custom-call(bf16[16,4,4096]{2,1,0:T(4,128)(2,1)} %vol_hbm.1, bf16[432,512]{1,0:T(8,128)(2,1)} %bitcast.2, bf16[32,2,1024]{2,1,0:T(2,128)(2,1)} %cot_hbm.1), custom_call_target="tpu_custom_call" | custom-call | tf_op jit(solution)/shard_map/pallas_call | solution.py:405
  50.0 2.2 %shard_map.59 = (bf16[32,2,1024]{2,1,0:T(2,128)(2,1)}, bf16[16,4,4096]{2,1,0:T(4,128)(2,1)}, f32[432,512]{1,0:T(8,128)}) custom-call(bf16[32,2,1024]{2,1,0:T(2,128)(2,1)} %get-tuple-element.9.act, bf16[16,4,4096]{2,1,0:T(4,128)(2,1)} %get-tuple-element.10.gvol, bf16[2,4,2,112,128]{4,3,2,1,0:T(8,128)(2,1)} %get-tuple-element.11.pieces), custom_call_target="tpu_custom_call" | custom-call | tf_op jit(solution)/shard_map/pallas_call | solution.py:421

commit v7 on v6

--- a/solution.py
+++ b/solution.py
@@ -269,12 +269,14 @@
         for side in range(2):
             filt[part, side, 0:ROWS, :] = total[:, side * PART : (side + 1) * PART]
         filt[part, :, ROWS:, :] = jnp.zeros((2, 4 * PIECE - ROWS, PART), F32)
-        filt_out[part] = filt[part].astype(BF)
         copies = []
-        for n, (dz, dy) in enumerate(deep + near):
-            start = pl.multiple_of(((y + dy) % 4) * PIECE, PIECE)
-            src = filt_out.at[part, (zh + dz) % 2, pl.ds(start, PIECE), :]
-            copies.append(push(src, filt_in.at[part, n], at_depth(dz, dy)))
+        for dz, group in ((1, deep), (0, near)):
+            half = (zh + dz) % 2
+            filt_out[part, half] = filt[part, half].astype(BF)
+            for _, dy in group:
+                start = pl.multiple_of(((y + dy) % 4) * PIECE, PIECE)
+                src = filt_out.at[part, half, pl.ds(start, PIECE), :]
+                copies.append(push(src, filt_in.at[part, len(copies)], at_depth(dz, dy)))
         return copies
 
     def summed(part, z, copies):

time: 52.8 us -> 52.9 us (level)
  no operation moved by 1% of the time
where the time goes in v7:
time: 52.9 us; the launch traced here: 52.2 us
  Pallas kernels  51.6 us (98%)
  between operations  0.64 us (1%)
    pallas_call x1, Pallas kernels, on_device(): pl.pallas_call(body, out_shape=(jax.ShapeDtypeStruct(cotangent.shape, BF)...  49.4 us
    pallas_call x1, Pallas kernels, on_device(): pl.pallas_call(store, out_shape=(jax.ShapeDtypeStruct(cotangent.shape, BF...  2.17 us

profile of v7, /device:TPU:1, one launch (start us, length us, event | category | flops | bytes accessed | tf_op | source)
XLA Modules:
  0.0 52.2 jit_solution(10136599816958966403)
XLA Ops:
  0.6 49.4 %shard_map.58 = (bf16[32,2,1024]{2,1,0:T(2,128)(2,1)}, bf16[16,4,4096]{2,1,0:T(4,128)(2,1)}, bf16[2,4,2,112,128]{4,3,2,1,0:T(8,128)(2,1)}) custom-call(bf16[16,4,4096]{2,1,0:T(4,128)(2,1)} %vol_hbm.1, bf16[432,512]{1,0:T(8,128)(2,1)} %bitcast.2, bf16[32,2,1024]{2,1,0:T(2,128)(2,1)} %cot_hbm.1), custom_call_target="tpu_custom_call" | custom-call | tf_op jit(solution)/shard_map/pallas_call | solution.py:407
  50.0 2.2 %shard_map.59 = (bf16[32,2,1024]{2,1,0:T(2,128)(2,1)}, bf16[16,4,4096]{2,1,0:T(4,128)(2,1)}, f32[432,512]{1,0:T(8,128)}) custom-call(bf16[32,2,1024]{2,1,0:T(2,128)(2,1)} %get-tuple-element.9.act, bf16[16,4,4096]{2,1,0:T(4,128)(2,1)} %get-tuple-element.10.gvol, bf16[2,4,2,112,128]{4,3,2,1,0:T(8,128)(2,1)} %get-tuple-element.11.pieces), custom_call_target="tpu_custom_call" | custom-call | tf_op jit(solution)/shard_map/pallas_call | solution.py:423
